TPU v7x, 32 devices: a whole 2x2x4 slice. The times are simulated.
32 devices in a mesh: cfg: 2 (over x), prow: 16 (over z, y, core).
Axes of the slice: x: 2, y: 2, z: 4, core: 2. Of those that a mesh axis runs over, the one named last changes fastest.
Arguments:
- top_panels: float32 [3072, 1536], P(('cfg', 'prow')), parts along dimension 0, may hold values from -0.15625 to 0.15625
- top_inverse: float32 [12, 256, 256], P('cfg'), parts along dimension 0, as said below
- pattern: int32 [64, 3], P('prow'), may hold values from 0 to 5, all different within a row
- child_blocks: float32 [128, 3, 256, 256], P(('cfg', 'prow')), parts along dimension 0, may hold values from -0.21875 to 0.21875
- child_inverse: float32 [128, 256, 256], P(('cfg', 'prow')), parts along dimension 0, as said below
Outputs:
- top_var: float32 [3072], P(('cfg', 'prow')), parts along dimension 0
- child_var: float32 [128, 256], P(('cfg', 'prow')), parts along dimension 0
There are 2 independent parts, one for each index of `cfg`. A program takes and returns all parts, laid end to end along the dimension named above; an argument that names none is the same for every part. Nothing has to cross between parts.
Inputs may be any that keep to these rules, and one draw needn't show every extreme that they name: `pattern`: each row names 3 different top supernodes; every top supernode is named by some row. `top_inverse`: each block is lower triangular with a positive diagonal. `child_inverse`: each block is lower triangular with a positive diagonal.
All inputs are finite; a program needn't handle non-finite values.
Results may differ from a plain program's by a relative error of at most 0.0001.
Values sent between devices are 32-bit elements; how exact they have to be, the bound alone decides.
A program may use at most 128 MiB of HBM per device.

v0:
```python
import functools

import jax
import jax.numpy as jnp
from jax import lax
from jax.experimental import pallas as pl
from jax.experimental.pallas import tpu as pltpu
from jax.sharding import PartitionSpec as P

F32 = jnp.float32
BF16 = jnp.bfloat16
MESH = pl.DeviceIdType.MESH


def split(x):
    high = x.astype(BF16)
    low = (x - high.astype(F32)).astype(BF16)
    return high, low


def mm(a, b):
    return jnp.dot(a, b, preferred_element_type=F32)


def mm3(ah, al, bh, bl):
    return mm(ah, bh) + mm(ah, bl) + mm(al, bh)


def kernel(
    n, nt, nb, rows, kids, links,
    panels_hbm, winv_hbm, pat, blocks_hbm, kinv_hbm,
    top_out, kid_out,
    pan, winv, blocks, kinv, w_h, w_l, wtw, sig_h, sig_l, u_h, u_l, kid_h, kid_f,
    own_sem, load_sem, recv_sem, up_sem, down_sem, y_sem, core_sem,
):
    cfg = lax.axis_index("cfg")
    me = lax.axis_index("prow")
    nz = n // 4
    z = me // 4
    y = (me // 2) % 2
    c = me % 2

    def index(zo, yo, co):
        return zo * 4 + yo * 2 + co

    y_peer = index(z, 1 - y, c)
    core_peer = index(z, y, 1 - c)
    below = index(jnp.maximum(z - 1, 0), y, c)
    above = index(jnp.minimum(z + 1, nz - 1), y, c)

    def needed(owner, k):
        return owner * rows + rows - 1 >= (k + 1) * nb

    own_copies = []
    for k in reversed(range(nt - 1)):
        copy = pltpu.make_async_copy(
            panels_hbm.at[:, k * nb:(k + 1) * nb],
            pan.at[k, pl.ds(me * rows, rows), :],
            own_sem.at[k],
        )
        copy.start()
        own_copies.append(copy)
    load_w = pltpu.make_async_copy(winv_hbm, winv, load_sem.at[0])
    load_v = pltpu.make_async_copy(kinv_hbm, kinv, load_sem.at[1])
    load_b = pltpu.make_async_copy(blocks_hbm, blocks, load_sem.at[2])
    load_w.start()
    load_v.start()
    load_b.start()

    barrier = pltpu.get_barrier_semaphore()
    for peer in (y_peer, core_peer):
        pl.semaphore_signal(barrier, inc=1, device_id=(cfg, peer), device_id_type=MESH)

    @pl.when(z > 0)
    def _():
        pl.semaphore_signal(barrier, inc=1, device_id=(cfg, below), device_id_type=MESH)

    @pl.when(z < nz - 1)
    def _():
        pl.semaphore_signal(barrier, inc=1, device_id=(cfg, above), device_id_type=MESH)

    peers = 2 + (z > 0).astype(jnp.int32) + (z < nz - 1).astype(jnp.int32)
    pl.semaphore_wait(barrier, peers)

    def piece(owner, k, peer, sem):
        part = pan.at[k, pl.ds(owner * rows, rows), :]
        return pltpu.make_async_remote_copy(
            src_ref=part, dst_ref=part, send_sem=sem, recv_sem=recv_sem.at[k, owner],
            device_id=(cfg, peer), device_id_type=MESH,
        )

    def recv(owner, k):
        piece(owner, k, core_peer, core_sem.at[k, 0, 0]).wait_recv()

    def column_copies(zo, k):
        owner = index(zo, y, c)
        return (
            (jnp.logical_and(zo >= z, z > 0), piece(owner, k, below, down_sem.at[k, zo])),
            (jnp.logical_and(zo <= z, z < nz - 1), piece(owner, k, above, up_sem.at[k, zo])),
            (None, piece(owner, k, y_peer, y_sem.at[k, zo])),
            (None, piece(owner, k, core_peer, core_sem.at[k, 0, zo])),
        )

    def for_column(zo, k, act):
        for cond, copy in column_copies(zo, k):
            if cond is None:
                act(copy)
            else:
                pl.when(cond)(functools.partial(act, copy))

    def start(copy):
        copy.start()

    def done(copy):
        copy.wait_send()

    def guarded(zo, yo, k, act):
        inside = jnp.logical_and(zo >= 0, zo < nz)
        pl.when(jnp.logical_and(inside, needed(index(zo, yo, c), k)))(act)

    def relay(k):
        def from_line(zo):
            def act():
                recv(index(zo, y, c), k)
                for_column(zo, k, start)
            guarded(zo, y, k, act)

        def from_y(zo):
            def act():
                owner = index(zo, 1 - y, c)
                recv(owner, k)
                piece(owner, k, core_peer, core_sem.at[k, 1, zo]).start()
            guarded(zo, 1 - y, k, act)

        def step(d, carry):
            from_line(z + d)
            from_line(z - d)
            @pl.when(d == 1)
            def _():
                from_y(z)

            @pl.when(d > 1)
            def _():
                from_y(z + d - 1)
                from_y(z - d + 1)
            return carry

        lax.fori_loop(1, nz, step, 0)
        from_y(z + nz - 1)
        from_y(z - nz + 1)

    def core_wait(k):
        def step(t, carry):
            owner = t * 2 + (1 - c)
            pl.when(needed(owner, k))(lambda: recv(owner, k))
            return carry
        lax.fori_loop(0, n // 2, step, 0)

    for copy, k in zip(own_copies, reversed(range(nt - 1))):
        copy.wait()

        @pl.when(needed(me, k))
        def _(k=k):
            for_column(z, k, start)

    load_w.wait()

    def prepare(k, carry):
        wh, wl = split(winv[k])
        w_h[k] = wh
        w_l[k] = wl
        th, tl = split(winv[k].T)
        wtw[k] = mm3(th, tl, wh, wl)
        return carry

    def kid_prepare(kid):
        vh, vl = split(kinv[kid])

        def step(i, carry):
            bh, bl = split(blocks[kid, i])
            value = mm3(bh, bl, vh, vl)
            high = value.astype(BF16)
            kid_h[kid, i] = high
            kid_f[kid, i] = 2.0 * value - high.astype(F32)
            return carry
        lax.fori_loop(0, links, step, 0)

    eye = (
        lax.broadcasted_iota(jnp.int32, (nb, nb), 0)
        == lax.broadcasted_iota(jnp.int32, (nb, nb), 1)
    )

    def set_diagonal(k, value):
        sig_h[k, k], sig_l[k, k] = split(value)
        top_out[k:k + 1, :] = jnp.sum(jnp.where(eye, value, 0.0), axis=0, keepdims=True)

    def column(k):
        after = range(k + 1, nt)

        def scale(r, carry):
            lh, ll = split(pan[k, pl.ds(r * nb, nb), :])
            value = mm3(lh, ll, w_h[k], w_l[k])
            u_h[r], u_l[r] = split(value)
            return carry
        lax.fori_loop(k + 1, nt, scale, 0)

        def row(i):
            total = None
            for j in after:
                term = mm3(sig_h[i, j], sig_l[i, j], u_h[j], u_l[j])
                total = term if total is None else total + term
            return total

        def fill(i, carry):
            value = -row(i)
            sig_h[i, k], sig_l[i, k] = split(value)
            sig_h[k, i], sig_l[k, i] = split(value.T)
            return carry
        lax.fori_loop(k + 1, nt, fill, 0)
        set_diagonal(k, wtw[k] - row(k))

    lax.fori_loop(0, nt, prepare, 0)
    set_diagonal(nt - 1, wtw[nt - 1])
    load_v.wait()
    load_b.wait()
    todo = list(range(kids))
    for k in reversed(range(nt - 1)):
        relay(k)
        if k + 1 < nt - 1:
            core_wait(k + 1)
            column(k + 1)
        if todo and k > 0:
            kid_prepare(todo.pop(0))
    for kid in todo:
        kid_prepare(kid)
    core_wait(0)
    column(0)

    def kid_finish(kid, carry):
        total = jnp.sum(kinv[kid] * kinv[kid], axis=0, keepdims=True)
        for i in range(links):
            coupled = None
            for j in range(links):
                bi, bj = pat[kid, i], pat[kid, j]
                term = mm(sig_h[bi, bj], kid_h[kid, j]) + mm(sig_l[bi, bj], kid_h[kid, j])
                coupled = term if coupled is None else coupled + term
            total = total + jnp.sum(kid_f[kid, i] * coupled, axis=0, keepdims=True)
        kid_out[pl.ds(kid, 1), :] = total
        return carry
    lax.fori_loop(0, kids, kid_finish, 0)

    for k in range(nt - 1):
        def finish(zo, carry, k=k):
            pl.when(needed(index(zo, y, c), k))(lambda: for_column(zo, k, done))

            @pl.when(needed(index(zo, 1 - y, c), k))
            def _():
                piece(index(zo, 1 - y, c), k, core_peer, core_sem.at[k, 1, zo]).wait_send()
            return carry
        lax.fori_loop(0, nz, finish, 0)


def local(n, top_panels, top_inverse, pattern, child_blocks, child_inverse):
    rows = top_panels.shape[0]
    nt, nb = top_inverse.shape[:2]
    kids, links = child_blocks.shape[:2]
    nz = n // 4
    dma = pltpu.SemaphoreType.DMA
    hbm = pl.BlockSpec(memory_space=pl.ANY)
    vmem = pl.BlockSpec(memory_space=pltpu.VMEM)
    diagonal, child_var = pl.pallas_call(
        functools.partial(kernel, n, nt, nb, rows, kids, links),
        out_shape=(
            jax.ShapeDtypeStruct((nt, nb), F32),
            jax.ShapeDtypeStruct((kids, nb), F32),
        ),
        in_specs=[hbm, hbm, pl.BlockSpec(memory_space=pltpu.SMEM), hbm, hbm],
        out_specs=(vmem, vmem),
        scratch_shapes=[
            pltpu.VMEM((nt - 1, nt * nb, nb), F32),
            pltpu.VMEM((nt, nb, nb), F32),
            pltpu.VMEM((kids, links, nb, nb), F32),
            pltpu.VMEM((kids, nb, nb), F32),
            pltpu.VMEM((nt, nb, nb), BF16),
            pltpu.VMEM((nt, nb, nb), BF16),
            pltpu.VMEM((nt, nb, nb), F32),
            pltpu.VMEM((nt, nt, nb, nb), BF16),
            pltpu.VMEM((nt, nt, nb, nb), BF16),
            pltpu.VMEM((nt, nb, nb), BF16),
            pltpu.VMEM((nt, nb, nb), BF16),
            pltpu.VMEM((kids, links, nb, nb), BF16),
            pltpu.VMEM((kids, links, nb, nb), F32),
            dma((nt - 1,)),
            dma((3,)),
            dma((nt - 1, n)),
            dma((nt - 1, nz)),
            dma((nt - 1, nz)),
            dma((nt - 1, nz)),
            dma((nt - 1, 2, nz)),
        ],
        compiler_params=pltpu.CompilerParams(
            collective_id=0, has_side_effects=True, vmem_limit_bytes=52 * 1024 * 1024,
        ),
    )(top_panels, top_inverse, pattern, child_blocks, child_inverse)
    first = lax.axis_index("prow") * rows
    top_var = lax.dynamic_slice_in_dim(diagonal.reshape(nt * nb), first, rows)
    return top_var, child_var


def solution(mesh):
    return jax.shard_map(
        functools.partial(local, mesh.shape["prow"]),
        mesh=mesh,
        in_specs=(
            P(("cfg", "prow"), None),
            P("cfg", None, None),
            P("prow", None),
            P(("cfg", "prow"), None, None, None),
            P(("cfg", "prow"), None, None),
        ),
        out_specs=(P(("cfg", "prow")), P(("cfg", "prow"), None)),
        check_vma=False,
    )
```

profile of v0, /device:TPU:0, one launch (start us, length us, event | category | flops | bytes accessed | tf_op | source)
XLA Modules:
  0.0 77.4 jit_solution(17294665385373171000)
XLA Ops:
  0.6 0.0 copy-start
  0.6 1.2 %copy-done = f32[4,256,256]{2,1,0:T(8,128)S(1)} copy-done((f32[4,256,256]{2,1,0:T(8,128)S(1)}, f32[4,256,256]{2,1,0:T(8,128)}, u32[]{:S(2)}) %copy-start) | copy-done | bytes 1048600
  1.9 0.0 copy-start.1
  1.9 1.1 %copy-done.1 = f32[96,1536]{1,0:T(8,128)S(1)} copy-done((f32[96,1536]{1,0:T(8,128)S(1)}, f32[96,1536]{1,0:T(8,128)}, u32[]{:S(2)}) %copy-start.1) | copy-done | bytes 589848
  2.9 0.0 copy-start.2
  2.9 0.7 copy-done.2
  3.6 72.6 %shard_map.68 = (f32[6,256]{1,0:T(8,128)S(1)}, f32[4,256]{1,0:T(4,128)S(1)}) custom-call(f32[96,1536]{1,0:T(8,128)S(1)} %copy-done.1, f32[6,256,256]{2,1,0:T(8,128)} %winv_hbm.1, s32[4,3]{1,0:T(4,128)S(1)} %copy-done.2, f32[4,3,256,256]{3,2,1,0:T(8,128)} %blocks_hbm.1, f32[4,256,256]{2,1,0:T(8,128)S(1)} %copy-done), custom_call_target="tpu_custom_call" | custom-call | tf_op jit(solution)/shard_map/pallas_call | solution.py:271
  76.2 0.6 dynamic_slice.3
  76.8 0.6 copy.8
  (1 shorter events, 0.0 us)
Async XLA Ops:
  0.6 1.2 %copy-start = (f32[4,256,256]{2,1,0:T(8,128)S(1)}, f32[4,256,256]{2,1,0:T(8,128)}, u32[]{:S(2)}) copy-start(f32[4,256,256]{2,1,0:T(8,128)} %kinv_hbm.1) | copy-start | bytes 3145732
  1.9 1.1 %copy-start.1 = (f32[96,1536]{1,0:T(8,128)S(1)}, f32[96,1536]{1,0:T(8,128)}, u32[]{:S(2)}) copy-start(f32[96,1536]{1,0:T(8,128)} %panels_hbm.1) | copy-start | bytes 1769476
  2.9 0.7 copy-start.2
where the time goes:
time: 77.6 us; the launch traced here: 77.4 us
  Pallas kernels  72.6 us (94%)
  local copies, waits for them, and re-layouts  4.15 us (5%)
    pallas_call x1, Pallas kernels, local(): pl.pallas_call(functools.partial(kernel, n, nt, nb, rows, kids, links), o...  72.6 us
    unnamed x7, local copies, waits for them, and re-layouts  3.55 us

commit v1 on v0

--- a/solution.py
+++ b/solution.py
@@ -31,7 +31,7 @@
     panels_hbm, winv_hbm, pat, blocks_hbm, kinv_hbm,
     top_out, kid_out,
     pan, winv, blocks, kinv, w_h, w_l, wtw, sig_h, sig_l, u_h, u_l, kid_h, kid_f,
-    own_sem, load_sem, recv_sem, up_sem, down_sem, y_sem, core_sem,
+    own_sem, load_sem, recv_sem, line_sem, down_sem, y_sem, core_sem,
 ):
     cfg = lax.axis_index("cfg")
     me = lax.axis_index("prow")
@@ -45,9 +45,6 @@
 
     y_peer = index(z, 1 - y, c)
     core_peer = index(z, y, 1 - c)
-    below = index(jnp.maximum(z - 1, 0), y, c)
-    above = index(jnp.minimum(z + 1, nz - 1), y, c)
-
     def needed(owner, k):
         return owner * rows + rows - 1 >= (k + 1) * nb
 
@@ -71,16 +68,15 @@
     for peer in (y_peer, core_peer):
         pl.semaphore_signal(barrier, inc=1, device_id=(cfg, peer), device_id_type=MESH)
 
-    @pl.when(z > 0)
-    def _():
-        pl.semaphore_signal(barrier, inc=1, device_id=(cfg, below), device_id_type=MESH)
-
-    @pl.when(z < nz - 1)
-    def _():
-        pl.semaphore_signal(barrier, inc=1, device_id=(cfg, above), device_id_type=MESH)
-
-    peers = 2 + (z > 0).astype(jnp.int32) + (z < nz - 1).astype(jnp.int32)
-    pl.semaphore_wait(barrier, peers)
+    def greet(zo, carry):
+        @pl.when(zo != z)
+        def _():
+            pl.semaphore_signal(
+                barrier, inc=1, device_id=(cfg, index(zo, y, c)), device_id_type=MESH
+            )
+        return carry
+    lax.fori_loop(0, nz, greet, 0)
+    pl.semaphore_wait(barrier, nz + 1)
 
     def piece(owner, k, peer, sem):
         part = pan.at[k, pl.ds(owner * rows, rows), :]
@@ -92,21 +88,25 @@
     def recv(owner, k):
         piece(owner, k, core_peer, core_sem.at[k, 0, 0]).wait_recv()
 
-    def column_copies(zo, k):
+    def for_own(k, act):
+        def to_line(zt):
+            @pl.when(jnp.logical_and(zt != z, jnp.logical_or(zt > 0, z < 2)))
+            def _():
+                act(piece(me, k, index(zt, y, c), line_sem.at[k, zt]))
+
+        def step(d, carry):
+            pl.when(z - d >= 0)(lambda: to_line(z - d))
+            pl.when(z + d < nz)(lambda: to_line(z + d))
+            return carry
+        lax.fori_loop(1, nz, step, 0)
+
+    def for_column(zo, k, act):
         owner = index(zo, y, c)
-        return (
-            (jnp.logical_and(zo >= z, z > 0), piece(owner, k, below, down_sem.at[k, zo])),
-            (jnp.logical_and(zo <= z, z < nz - 1), piece(owner, k, above, up_sem.at[k, zo])),
-            (None, piece(owner, k, y_peer, y_sem.at[k, zo])),
-            (None, piece(owner, k, core_peer, core_sem.at[k, 0, zo])),
-        )
-
-    def for_column(zo, k, act):
-        for cond, copy in column_copies(zo, k):
-            if cond is None:
-                act(copy)
-            else:
-                pl.when(cond)(functools.partial(act, copy))
+        @pl.when(jnp.logical_and(z == 1, zo > 1))
+        def _():
+            act(piece(owner, k, index(0, y, c), down_sem.at[k, zo]))
+        act(piece(owner, k, y_peer, y_sem.at[k, zo]))
+        act(piece(owner, k, core_peer, core_sem.at[k, 0, zo]))
 
     def start(copy):
         copy.start()
@@ -114,40 +114,41 @@
     def done(copy):
         copy.wait_send()
 
-    def guarded(zo, yo, k, act):
+    def highest(owner):
+        return (owner * rows + rows - 1) // nb - 1
+
+    def guarded(zo, yo, s, act):
+        owner = index(zo, yo, c)
         inside = jnp.logical_and(zo >= 0, zo < nz)
-        pl.when(jnp.logical_and(inside, needed(index(zo, yo, c), k)))(act)
-
-    def relay(k):
+        pl.when(jnp.logical_and(inside, highest(owner) >= s))(lambda: act(owner, highest(owner) - s))
+
+    def line_relay(s):
         def from_line(zo):
-            def act():
-                recv(index(zo, y, c), k)
+            def act(owner, k):
+                recv(owner, k)
                 for_column(zo, k, start)
-            guarded(zo, y, k, act)
-
-        def from_y(zo):
-            def act():
-                owner = index(zo, 1 - y, c)
-                recv(owner, k)
-                piece(owner, k, core_peer, core_sem.at[k, 1, zo]).start()
-            guarded(zo, 1 - y, k, act)
+            guarded(zo, y, s, act)
 
         def step(d, carry):
             from_line(z + d)
             from_line(z - d)
-            @pl.when(d == 1)
-            def _():
-                from_y(z)
-
-            @pl.when(d > 1)
-            def _():
-                from_y(z + d - 1)
-                from_y(z - d + 1)
             return carry
 
         lax.fori_loop(1, nz, step, 0)
-        from_y(z + nz - 1)
-        from_y(z - nz + 1)
+
+    def y_relay(s):
+        def from_y(zo):
+            def act(owner, k):
+                recv(owner, k)
+                piece(owner, k, core_peer, core_sem.at[k, 1, zo]).start()
+            guarded(zo, 1 - y, s, act)
+
+        def step(d, carry):
+            from_y(z + d)
+            pl.when(d > 0)(lambda: from_y(z - d))
+            return carry
+
+        lax.fori_loop(0, nz, step, 0)
 
     def core_wait(k):
         def step(t, carry):
@@ -156,12 +157,13 @@
             return carry
         lax.fori_loop(0, n // 2, step, 0)
 
-    for copy, k in zip(own_copies, reversed(range(nt - 1))):
+    for copy in own_copies:
         copy.wait()
-
-        @pl.when(needed(me, k))
-        def _(k=k):
+    for s in range(nt - 1):
+        def issue(owner, k):
+            for_own(k, start)
             for_column(z, k, start)
+        guarded(z, y, s, issue)
 
     load_w.wait()
 
@@ -224,15 +226,22 @@
     load_v.wait()
     load_b.wait()
     todo = list(range(kids))
-    for k in reversed(range(nt - 1)):
-        relay(k)
-        if k + 1 < nt - 1:
-            core_wait(k + 1)
-            column(k + 1)
-        if todo and k > 0:
+    last = nt - 2
+    for s in range(nt - 1):
+        k = last - s
+        line_relay(s)
+        if s >= 1:
+            y_relay(s - 1)
+        if s >= 2:
+            core_wait(k + 2)
+            column(k + 2)
+        elif todo:
             kid_prepare(todo.pop(0))
     for kid in todo:
         kid_prepare(kid)
+    core_wait(1)
+    column(1)
+    y_relay(last)
     core_wait(0)
     column(0)
 
@@ -250,6 +259,8 @@
     lax.fori_loop(0, kids, kid_finish, 0)
 
     for k in range(nt - 1):
+        pl.when(needed(me, k))(lambda k=k: for_own(k, done))
+
         def finish(zo, carry, k=k):
             pl.when(needed(index(zo, y, c), k))(lambda: for_column(zo, k, done))
 
@@ -299,7 +310,7 @@
             dma((nt - 1, 2, nz)),
         ],
         compiler_params=pltpu.CompilerParams(
-            collective_id=0, has_side_effects=True, vmem_limit_bytes=52 * 1024 * 1024,
+            collective_id=0, has_side_effects=True, vmem_limit_bytes=60 * 1024 * 1024,
         ),
     )(top_panels, top_inverse, pattern, child_blocks, child_inverse)
     first = lax.axis_index("prow") * rows

time: 77.6 us -> 61.5 us (0.79); the launches traced: 77.4 us -> 60.5 us
  Pallas kernels: 72.6 us -> 57.3 us
  local copies, waits for them, and re-layouts: 4.15 us -> 2.55 us
    pallas_call x1, Pallas kernels: 72.6 us -> 57.3 us  [local(): pl.pallas_call(functools.partial(kernel, n, nt, nb, rows, kids, links), o...]
    unnamed x7 -> x1, local copies, waits for them, and re-layouts: 3.55 us -> 1.26 us
where the time goes in v1:
time: 61.5 us; the launch traced here: 60.5 us
  Pallas kernels  57.3 us (93%)
  local copies, waits for them, and re-layouts  2.55 us (4%)
  between operations  0.64 us (1%)
    pallas_call x1, Pallas kernels, local(): pl.pallas_call(functools.partial(kernel, n, nt, nb, rows, kids, links), o...  57.3 us
    unnamed x1, local copies, waits for them, and re-layouts  1.26 us

profile of v1, /device:TPU:0, one launch (start us, length us, event | category | flops | bytes accessed | tf_op | source)
XLA Modules:
  0.0 60.5 jit_solution(1675279160889734022)
XLA Ops:
  0.6 57.3 %shard_map.68 = (f32[6,256]{1,0:T(8,128)}, f32[4,256]{1,0:T(4,128)}) custom-call(f32[96,1536]{1,0:T(8,128)} %panels_hbm.1, f32[6,256,256]{2,1,0:T(8,128)} %winv_hbm.1, s32[4,3]{1,0:T(4,128)} %pat.1, f32[4,3,256,256]{3,2,1,0:T(8,128)} %blocks_hbm.1, f32[4,256,256]{2,1,0:T(8,128)} %kinv_hbm.1), custom_call_target="tpu_custom_call" | custom-call | tf_op jit(solution)/shard_map/pallas_call | solution.py:282
  57.9 0.7 %reshape.7 = f32[1536]{0:T(1024)S(1)} reshape(f32[6,256]{1,0:T(8,128)} %get-tuple-element.4) | data formatting | bytes 12288 | tf_op jit(solution)/shard_map/reshape | solution.py:317
  58.6 0.6 dynamic_slice.3
  59.2 1.3 %copy.8 = f32[4,256]{1,0:T(4,128)} copy(f32[4,256]{1,0:T(4,128)} %get-tuple-element.9) | data formatting | bytes 8192

commit v2 on v1

--- a/solution.py
+++ b/solution.py
@@ -60,9 +60,6 @@
     load_w = pltpu.make_async_copy(winv_hbm, winv, load_sem.at[0])
     load_v = pltpu.make_async_copy(kinv_hbm, kinv, load_sem.at[1])
     load_b = pltpu.make_async_copy(blocks_hbm, blocks, load_sem.at[2])
-    load_w.start()
-    load_v.start()
-    load_b.start()
 
     barrier = pltpu.get_barrier_semaphore()
     for peer in (y_peer, core_peer):
@@ -165,6 +162,9 @@
             for_column(z, k, start)
         guarded(z, y, s, issue)
 
+    load_w.start()
+    load_v.start()
+    load_b.start()
     load_w.wait()
 
     def prepare(k, carry):
@@ -185,7 +185,7 @@
             kid_h[kid, i] = high
             kid_f[kid, i] = 2.0 * value - high.astype(F32)
             return carry
-        lax.fori_loop(0, links, step, 0)
+        lax.fori_loop(0, links, step, 0, unroll=True)
 
     eye = (
         lax.broadcasted_iota(jnp.int32, (nb, nb), 0)
@@ -204,7 +204,7 @@
             value = mm3(lh, ll, w_h[k], w_l[k])
             u_h[r], u_l[r] = split(value)
             return carry
-        lax.fori_loop(k + 1, nt, scale, 0)
+        lax.fori_loop(k + 1, nt, scale, 0, unroll=True)
 
         def row(i):
             total = None
@@ -218,7 +218,7 @@
             sig_h[i, k], sig_l[i, k] = split(value)
             sig_h[k, i], sig_l[k, i] = split(value.T)
             return carry
-        lax.fori_loop(k + 1, nt, fill, 0)
+        lax.fori_loop(k + 1, nt, fill, 0, unroll=True)
         set_diagonal(k, wtw[k] - row(k))
 
     lax.fori_loop(0, nt, prepare, 0)
@@ -239,9 +239,9 @@
             kid_prepare(todo.pop(0))
     for kid in todo:
         kid_prepare(kid)
+    y_relay(last)
     core_wait(1)
     column(1)
-    y_relay(last)
     core_wait(0)
     column(0)
 

time: 61.5 us -> 54.7 us (0.89); the launches traced: 60.5 us -> 54.5 us
  Pallas kernels: 57.3 us -> 51.3 us
    pallas_call x1, Pallas kernels: 57.3 us -> 51.3 us  [local(): pl.pallas_call(functools.partial(kernel, n, nt, nb, rows, kids, links), o...]
where the time goes in v2:
time: 54.7 us; the launch traced here: 54.5 us
  Pallas kernels  51.3 us (94%)
  local copies, waits for them, and re-layouts  2.55 us (5%)
  between operations  0.64 us (1%)
    pallas_call x1, Pallas kernels, local(): pl.pallas_call(functools.partial(kernel, n, nt, nb, rows, kids, links), o...  51.3 us
    unnamed x1, local copies, waits for them, and re-layouts  1.26 us

profile of v2, /device:TPU:0, one launch (start us, length us, event | category | flops | bytes accessed | tf_op | source)
XLA Modules:
  0.0 54.5 jit_solution(5615734716421286542)
XLA Ops:
  0.6 51.3 %shard_map.68 = (f32[6,256]{1,0:T(8,128)}, f32[4,256]{1,0:T(4,128)}) custom-call(f32[96,1536]{1,0:T(8,128)} %panels_hbm.1, f32[6,256,256]{2,1,0:T(8,128)} %winv_hbm.1, s32[4,3]{1,0:T(4,128)} %pat.1, f32[4,3,256,256]{3,2,1,0:T(8,128)} %blocks_hbm.1, f32[4,256,256]{2,1,0:T(8,128)} %kinv_hbm.1), custom_call_target="tpu_custom_call" | custom-call | tf_op jit(solution)/shard_map/pallas_call | solution.py:282
  51.9 0.7 %reshape.7 = f32[1536]{0:T(1024)S(1)} reshape(f32[6,256]{1,0:T(8,128)} %get-tuple-element.4) | data formatting | bytes 12288 | tf_op jit(solution)/shard_map/reshape | solution.py:317
  52.6 0.6 %dynamic_slice.3 = f32[96]{0:T(128)} dynamic-slice(f32[1536]{0:T(1024)S(1)} %reshape.7, s32[]{:T(128)S(6)} %select_n.3), dynamic_slice_sizes={96} | dynamic-slice | bytes 772 | tf_op jit(solution)/shard_map/dynamic_slice | solution.py:317
  53.2 1.3 %copy.8 = f32[4,256]{1,0:T(4,128)} copy(f32[4,256]{1,0:T(4,128)} %get-tuple-element.9) | data formatting | bytes 8192
